TPU v7x, 512 devices: a whole 4x4x16 slice. The times are simulated.
512 devices in a mesh: vocab: 32 (over x, y, core), dp: 16 (over z).
Axes of the slice: x: 4, y: 4, z: 16, core: 2. Of those that a mesh axis runs over, the one named last changes fastest.
Arguments:
- hidden: bfloat16 [2048, 2048], P('dp', 'vocab')
- head_weight: bfloat16 [2048, 65536], P('dp', 'vocab')
- teacher_logits: bfloat16 [2048, 65536], P('dp', 'vocab')
- target_ids: int32 [2048], P('dp'), may hold values from 0 to 65535
- segment_ids: int32 [16, 128], P('dp'), may hold values from 0 to 15, never falling along the last dimension, each value on 1 to 16 neighbouring positions
- pair_order: int32 [16, 16], P('dp'), may hold values from 0 to 15, each once within a row
Outputs:
- hidden_grad: bfloat16 [2048, 2048], P('dp', 'vocab')
- head_grad: float32 [2048, 65536], P('dp', 'vocab')
- loss: float32 [], replicated
Inputs may be any that keep to these rules, and one draw needn't show every extreme that they name: `segment_ids`: in each group the row's sequence number never falls along the rows, and every sequence has 1 to 16 rows. `pair_order`: each group's row is a permutation of its 16 sequences; pair p is entry 2p (chosen) and entry 2p + 1 (rejected).
All inputs are finite; a program needn't handle non-finite values.
Results may differ from a plain program's by a relative error of at most 0.018.
Values may be sent and summed in bfloat16 or wider, within the bound.
No kernel may reach another device: no remote copies, remote signals or barrier semaphores. Data moves between devices by JAX's collectives and lax.ppermute only.
A program may use at most 64 MiB of HBM per device.

v0:
```python
import jax
import jax.numpy as jnp
from jax import lax
from jax.sharding import PartitionSpec as P

dpo_beta = 0.1
dpo_gamma = 4.0


def pair_weights(log_ratio, segments, ordering):
    seq_count = ordering.shape[0]
    labels = lax.broadcasted_iota(jnp.int32, (1, seq_count), 1)
    seq_hot = (segments[:, None] == labels).astype(jnp.float32)
    seq_ratio = jnp.sum(seq_hot * log_ratio[:, None], axis=0)
    chosen = ordering[0::2]
    rejected = ordering[1::2]
    chosen_hot = (chosen[:, None] == labels).astype(jnp.float32)
    rejected_hot = (rejected[:, None] == labels).astype(jnp.float32)
    margin = dpo_beta * (
        jnp.sum(chosen_hot * seq_ratio[None, :], axis=1)
        - jnp.sum(rejected_hot * seq_ratio[None, :], axis=1)
    )
    strength = dpo_gamma * dpo_beta * jax.nn.sigmoid(-margin)
    coeffs = jnp.sum((rejected_hot - chosen_hot) * strength[:, None], axis=0)
    row_weight = jnp.sum(seq_hot * coeffs[None, :], axis=1)
    return (row_weight, jnp.sum(jax.nn.softplus(-margin)))


def to_all(block, axis):
    count = lax.axis_size(axis)
    copies = jnp.broadcast_to(block[None], (count,) + block.shape)
    return lax.all_to_all(copies, axis, 0, 0, tiled=True)


def on_device(hidden, head_weight, teacher_logits, target_ids, segment_ids, pair_order):
    f32, bf16 = (jnp.float32, jnp.bfloat16)
    rows_full = lax.all_gather(hidden, "vocab", axis=1, tiled=True)
    width = head_weight.shape[1]
    half = width // 2
    weight_lo = lax.all_gather(head_weight[:, :half], "dp", axis=0, tiled=True)
    weight_hi = lax.all_gather(head_weight[:, half:], "dp", axis=0, tiled=True)
    student = jnp.concatenate(
        [
            jnp.dot(rows_full, weight_lo, preferred_element_type=f32),
            jnp.dot(rows_full, weight_hi, preferred_element_type=f32),
        ],
        axis=1,
    )
    teacher = teacher_logits.astype(f32)
    n_vocab = lax.axis_size("vocab")
    n_dp = lax.axis_size("dp")
    rows = student.shape[0]
    offset = lax.axis_index("vocab") * width
    column = lax.broadcasted_iota(jnp.int32, student.shape, 1) + offset
    is_target = column == target_ids[:, None]
    own_max = jnp.max(student, axis=1)
    own_tmax = jnp.max(teacher, axis=1)
    own_exp = jnp.exp(student - own_max[:, None])
    own_texp = jnp.exp(teacher - own_tmax[:, None])
    stats = jnp.stack(
        [
            own_max,
            own_tmax,
            jnp.sum(own_exp, axis=1),
            jnp.sum(own_texp, axis=1),
            jnp.sum(own_texp * (teacher - student), axis=1),
            jnp.sum(jnp.where(is_target, student, 0.0), axis=1),
            jnp.sum(jnp.where(is_target, teacher, 0.0), axis=1),
            jnp.zeros((rows,), f32),
        ]
    )
    every = to_all(stats, "vocab").reshape(n_vocab, 8, rows)
    max_student = jnp.max(every[:, 0], axis=0)
    max_teacher = jnp.max(every[:, 1], axis=0)
    scale_s = jnp.exp(every[:, 0] - max_student[None])
    scale_t = jnp.exp(every[:, 1] - max_teacher[None])
    sum_student = jnp.sum(every[:, 2] * scale_s, axis=0)
    sum_teacher = jnp.sum(every[:, 3] * scale_t, axis=0)
    cross = jnp.sum(every[:, 4] * scale_t, axis=0)
    target_student = jnp.sum(every[:, 5], axis=0)
    target_teacher = jnp.sum(every[:, 6], axis=0)
    lse_student = max_student + jnp.log(sum_student)
    lse_teacher = max_teacher + jnp.log(sum_teacher)
    kl_rows = cross / sum_teacher - lse_teacher + lse_student
    log_ratio = target_student - lse_student - (target_teacher - lse_teacher)
    row_weight, dpo_sum = pair_weights(log_ratio, segment_ids[0], pair_order[0])
    group_objective = jnp.sum(kl_rows) + dpo_gamma * dpo_sum
    exp_student = jnp.exp(student - max_student[:, None])
    exp_teacher = jnp.exp(teacher - max_teacher[:, None])
    prob_student = exp_student / sum_student[:, None]
    prob_teacher = exp_teacher / sum_teacher[:, None]
    logit_grad = (
        prob_student - prob_teacher + row_weight[:, None] * (is_target.astype(f32) - prob_student)
    ).astype(bf16)
    grad_lo = logit_grad[:, :half]
    grad_hi = logit_grad[:, half:]
    all_lo = lax.all_gather(grad_lo, "dp", axis=0, tiled=True)
    all_hi = lax.all_gather(grad_hi, "dp", axis=0, tiled=True)
    nt = (((1,), (1,)), ((), ()))
    hidden_term = (
        lax.dot_general(grad_lo, weight_lo, nt, preferred_element_type=f32)
        + lax.dot_general(grad_hi, weight_hi, nt, preferred_element_type=f32)
    ).astype(bf16)
    feats = hidden_term.shape[1] // n_vocab
    terms = hidden_term.reshape(rows, n_vocab, feats).swapaxes(0, 1)
    terms = lax.all_to_all(terms, "vocab", 0, 0, tiled=True)
    hidden_grad = jnp.sum(terms.astype(f32), axis=0).astype(bf16)
    objectives = to_all(jnp.full((8, 128), group_objective, f32), "dp").reshape(n_dp, 8, 128)
    loss_value = jnp.sum(objectives[:, 0, 0]) / (rows * n_dp)
    grad_cols = lax.all_to_all(rows_full, "dp", split_axis=1, concat_axis=0, tiled=True)
    tn = (((0,), (0,)), ((), ()))
    head_grad = jnp.concatenate(
        [
            lax.dot_general(grad_cols, all_lo, tn, preferred_element_type=f32),
            lax.dot_general(grad_cols, all_hi, tn, preferred_element_type=f32),
        ],
        axis=1,
    )
    return (hidden_grad, head_grad, loss_value)


def solution(mesh):
    return jax.shard_map(
        on_device,
        mesh=mesh,
        in_specs=(
            P("dp", "vocab"),
            P("dp", "vocab"),
            P("dp", "vocab"),
            P("dp"),
            P("dp", None),
            P("dp", None),
        ),
        out_specs=(P("dp", "vocab"), P("dp", "vocab"), P()),
        check_vma=False,
    )
```

profile of v0, /device:TPU:2, one launch (start us, length us, event | category | flops | bytes accessed | tf_op | source)
XLA Modules:
  0.0 374.6 jit_solution(1377167011678018934)
XLA Ops:
  7.2 0.0 all-gather.5.cloned.1.call-start
  7.2 1.8 fusion.19
  9.0 0.0 all-gather.5.cloned.1.call-update
  9.1 0.0 all-gather.7.cloned.1.call-start
  9.1 0.7 all-gather.7.cloned.1.call-update
  9.8 1.2 reduce_max.71
  11.0 29.9 %all_gather.15 = bf16[128,2048]{0,1:T(8,128)(2,1)} all-gather(bf16[128,64]{0,1:T(8,128)(2,1)} %param.6), channel_id=1, replica_groups=mesh['vocab'=32,'dp'=16] {'vocab'}, dimensions={1}, use_global_device_ids=true | all-gather | bytes 540672 | tf_op jit(solution)/shard_map/all_gather | solution.py:37
  40.9 0.0 copy-start
  40.9 0.0 copy-start.1
  40.9 52.3 %all-gather.5.cloned.1.call-done = bf16[2048,1024]{1,0:T(8,128)(2,1)} async-done(((bf16[128,1024]{1,0:T(8,128)(2,1)}), bf16[2048,1024]{1,0:T(8,128)(2,1)}) %all-gather.5.cloned.1.call-update) | async-done | bytes 4194320 | tf_op jit(solution)/shard_map/all_gather | solution.py:40
  93.3 3.2 fusion.22
  96.4 0.0 copy-start.2
  96.5 0.0 copy-start.3
  96.5 74.8 %all-gather.7.cloned.1.call-done = bf16[2048,1024]{1,0:T(8,128)(2,1)} async-done(((bf16[128,1024]{1,0:T(8,128)(2,1)}), bf16[2048,1024]{1,0:T(8,128)(2,1)}) %all-gather.7.cloned.1.call-update) | async-done | bytes 4194320 | tf_op jit(solution)/shard_map/all_gather | solution.py:41
  171.3 3.2 fusion.23
  174.5 0.0 copy-done
  174.5 0.0 copy-done.1
  174.5 0.8 fusion.1
  175.4 0.7 broadcast_in_dim.8
  176.0 7.4 %all-to-all-start = ((f32[32,8,128]{2,1,0:T(8,128)}), f32[32,8,128]{2,1,0:T(8,128)S(1)}, u32[]{:S(2)}, u32[]{:S(2)}) async-start(f32[32,8,128]{2,1,0:T(8,128)} %broadcast_in_dim.8), calls=%async_computation | async-start | bytes 262144 | tf_op jit(solution)/shard_map/all_to_all | solution.py:32
  183.5 0.0 all-gather.9.cloned.1.call-start
  183.5 0.0 copy-done.2
  183.5 0.1 slice.51
  183.6 0.1 slice.50
  183.7 6.4 %all-to-all-done = f32[32,8,128]{2,1,0:T(8,128)S(1)} async-done(((f32[32,8,128]{2,1,0:T(8,128)}), f32[32,8,128]{2,1,0:T(8,128)S(1)}, u32[]{:S(2)}, u32[]{:S(2)}) %all-to-all-start) | async-done | bytes 131104 | tf_op jit(solution)/shard_map/all_to_all | solution.py:32
  190.1 0.1 fusion.20
  190.3 0.6 add_reduce_fusion
  190.9 0.0 copy-done.3
  190.9 0.1 select_reduce_fusion.1
  191.0 0.2 select_reduce_fusion.2
  191.3 0.6 fusion.14
  191.9 0.1 multiply_reduce_fusion.3
  192.0 0.1 select_reduce_fusion
  192.1 0.6 fusion.5
  192.7 0.9 fusion.18
  193.5 0.0 all-gather.9.cloned.1.call-update
  193.6 0.0 all-gather.11.cloned.1.call-start
  193.6 0.5 all-gather.11.cloned.1.call-update
  194.1 7.4 %all-to-all-start.2 = ((bf16[128,16,128]{0,2,1:T(8,128)(2,1)}), bf16[128,16,128]{0,2,1:T(8,128)(2,1)S(1)}, u32[]{:S(2)}, u32[]{:S(2)}) async-start(bf16[128,16,128]{0,2,1:T(8,128)(2,1)} %bitcast.17), calls=%async_computation.2 | async-start | bytes 1048576 | tf_op jit(solution)/shard_map/all_to_all | solution.py:110
  202.9 3.8 %fusion.16 = f32[128,2048]{1,0:T(8,128)S(1)} fusion(bf16[2048,1024]{1,0:T(8,128)(2,1)} %all-gather.5.cloned.1.call-done, bf16[128,2048]{1,0:T(8,128)(2,1)S(1)} %fusion.5), kind=kOutput, calls=%fused_computation.50 | convolution fusion | flops 536870912 | bytes 5505024 | tf_op jit(solution)/shard_map/dot_general | solution.py:101
  206.7 29.5 %all-to-all-done.2 = bf16[128,16,128]{0,2,1:T(8,128)(2,1)S(1)} async-done(((bf16[128,16,128]{0,2,1:T(8,128)(2,1)}), bf16[128,16,128]{0,2,1:T(8,128)(2,1)S(1)}, u32[]{:S(2)}, u32[]{:S(2)}) %all-to-all-start.2) | async-done | bytes 524320 | tf_op jit(solution)/shard_map/all_to_all | solution.py:110
  236.2 0.6 broadcast_in_dim_broadcast_in_dim_broadcast_in_dim.3
  236.8 6.4 %all-to-all-start.3 = ((f32[16,8,128]{2,1,0:T(8,128)}), f32[16,8,128]{2,1,0:T(8,128)S(1)}, u32[]{:S(2)}, u32[]{:S(2)}) async-start(f32[16,8,128]{2,1,0:T(8,128)} %broadcast_in_dim_broadcast_in_dim_broadcast_in_dim.3), calls=%async_computation.3 | async-start | bytes 131072 | tf_op jit(solution)/shard_map/all_to_all | solution.py:32
  243.2 3.7 fusion
  246.9 1.0 copy.32
  247.9 8.8 %all-to-all-done.3 = f32[16,8,128]{2,1,0:T(8,128)S(1)} async-done(((f32[16,8,128]{2,1,0:T(8,128)}), f32[16,8,128]{2,1,0:T(8,128)S(1)}, u32[]{:S(2)}, u32[]{:S(2)}) %all-to-all-start.3) | async-done | bytes 65568 | tf_op jit(solution)/shard_map/all_to_all | solution.py:32
  256.8 5.0 %all-to-all-start.1 = ((bf16[32,128,64]{1,2,0:T(8,128)(2,1)}), bf16[32,128,64]{1,2,0:T(8,128)(2,1)S(1)}, u32[]{:S(2)}, u32[]{:S(2)}) async-start(bf16[32,128,64]{1,2,0:T(8,128)(2,1)} %bitcast.16), calls=%async_computation.1 | async-start | bytes 1048576 | tf_op jit(solution)/shard_map/all_to_all | solution.py:106
  261.8 0.3 copy.33
  262.1 0.6 slice_reduce_fusion
  263.4 8.2 %all-to-all-done.1 = bf16[32,128,64]{1,2,0:T(8,128)(2,1)S(1)} async-done(((bf16[32,128,64]{1,2,0:T(8,128)(2,1)}), bf16[32,128,64]{1,2,0:T(8,128)(2,1)S(1)}, u32[]{:S(2)}, u32[]{:S(2)}) %all-to-all-start.1) | async-done | bytes 524320 | tf_op jit(solution)/shard_map/all_to_all | solution.py:106
  271.5 0.7 reduce_sum.188
  272.2 15.8 %all-gather.9.cloned.1.call-done = bf16[2048,1024]{1,0:T(8,128)(2,1)} async-done(((bf16[128,1024]{1,0:T(8,128)(2,1)}), bf16[2048,1024]{1,0:T(8,128)(2,1)}) %all-gather.9.cloned.1.call-update) | async-done | bytes 4194320 | tf_op jit(solution)/shard_map/all_gather | solution.py:97
  288.0 3.5 convolution_bitcast_fusion.1
  291.5 70.6 %all-gather.11.cloned.1.call-done = bf16[2048,1024]{1,0:T(8,128)(2,1)} async-done(((bf16[128,1024]{1,0:T(8,128)(2,1)}), bf16[2048,1024]{1,0:T(8,128)(2,1)}) %all-gather.11.cloned.1.call-update) | async-done | bytes 4194320 | tf_op jit(solution)/shard_map/all_gather | solution.py:98
  362.1 3.5 convolution_bitcast_fusion
  365.5 0.1 pad_maximum_fusion.1
  365.6 1.3 copy.35
  (10 shorter events, 0.2 us)
Async XLA Ops:
  7.2 86.1 %all-gather.5.cloned.1.call-start = ((), (), s32[]{:S(2)}) async-start(), calls=%async_computation.4 | async-start | bytes 4456448 | tf_op jit(solution)/shard_map/all_gather | solution.py:40
  9.1 162.2 %all-gather.7.cloned.1.call-start = ((), (), s32[]{:S(2)}) async-start(), calls=%async_computation.5 | async-start | bytes 4456448 | tf_op jit(solution)/shard_map/all_gather | solution.py:41
  40.9 133.6 %copy-start = (bf16[128,2048]{1,0:T(8,128)(2,1)S(1)}, bf16[128,2048]{1,0:T(8,128)(2,1)}, u32[]{:S(2)}) copy-start(bf16[128,2048]{1,0:T(8,128)(2,1)} %param.8) | copy-start | bytes 1572868
  40.9 133.6 %copy-start.1 = (s32[128]{0:T(128)S(1)}, s32[128]{0:T(128)}, u32[]{:S(2)}) copy-start(s32[128]{0:T(128)} %param.9) | copy-start | bytes 1540
  96.4 87.1 %copy-start.2 = (s32[1,16]{1,0:T(1,128)S(1)}, s32[1,16]{1,0:T(1,128)}, u32[]{:S(2)}) copy-start(s32[1,16]{1,0:T(1,128)} %param.11) | copy-start | bytes 196
  96.5 94.5 %copy-start.3 = (s32[1,128]{1,0:T(1,128)S(1)}, s32[1,128]{1,0:T(1,128)}, u32[]{:S(2)}) copy-start(s32[1,128]{1,0:T(1,128)} %param.10) | copy-start | bytes 1540
  176.0 14.1 %all-to-all-start = ((f32[32,8,128]{2,1,0:T(8,128)}), f32[32,8,128]{2,1,0:T(8,128)S(1)}, u32[]{:S(2)}, u32[]{:S(2)}) async-start(f32[32,8,128]{2,1,0:T(8,128)} %broadcast_in_dim.8), calls=%async_computation | async-start | bytes 262144 | tf_op jit(solution)/shard_map/all_to_all | solution.py:32
  183.5 104.5 %all-gather.9.cloned.1.call-start = ((), (), s32[]{:S(2)}) async-start(), calls=%async_computation.6 | async-start | bytes 4456448 | tf_op jit(solution)/shard_map/all_gather | solution.py:97
  193.6 168.5 %all-gather.11.cloned.1.call-start = ((), (), s32[]{:S(2)}) async-start(), calls=%async_computation.7 | async-start | bytes 4456448 | tf_op jit(solution)/shard_map/all_gather | solution.py:98
  194.1 42.0 %all-to-all-start.2 = ((bf16[128,16,128]{0,2,1:T(8,128)(2,1)}), bf16[128,16,128]{0,2,1:T(8,128)(2,1)S(1)}, u32[]{:S(2)}, u32[]{:S(2)}) async-start(bf16[128,16,128]{0,2,1:T(8,128)(2,1)} %bitcast.17), calls=%async_computation.2 | async-start | bytes 1048576 | tf_op jit(solution)/shard_map/all_to_all | solution.py:110
  236.8 20.0 %all-to-all-start.3 = ((f32[16,8,128]{2,1,0:T(8,128)}), f32[16,8,128]{2,1,0:T(8,128)S(1)}, u32[]{:S(2)}, u32[]{:S(2)}) async-start(f32[16,8,128]{2,1,0:T(8,128)} %broadcast_in_dim_broadcast_in_dim_broadcast_in_dim.3), calls=%async_computation.3 | async-start | bytes 131072 | tf_op jit(solution)/shard_map/all_to_all | solution.py:32
  256.8 14.8 %all-to-all-start.1 = ((bf16[32,128,64]{1,2,0:T(8,128)(2,1)}), bf16[32,128,64]{1,2,0:T(8,128)(2,1)S(1)}, u32[]{:S(2)}, u32[]{:S(2)}) async-start(bf16[32,128,64]{1,2,0:T(8,128)(2,1)} %bitcast.16), calls=%async_computation.1 | async-start | bytes 1048576 | tf_op jit(solution)/shard_map/all_to_all | solution.py:106
Sparse Core Ops, SparseCore 0:
  10.1 83.1 all-gather.4
  95.9 75.3 all-gather.6
  193.7 94.2 all-gather.8
  289.9 72.1 all-gather.10
where the time goes:
time: 375 us
  waiting for transfers between devices  268 us (71%)
  blocking collectives  29.9 us (8%)
  starting transfers between devices  26.5 us (7%)
  matrix products  20.8 us (6%)
  between operations  17 us (5%)
  local copies, waits for them, and re-layouts  6.89 us (2%)
  other arithmetic  5.88 us (2%)
    all_gather x1, waiting for transfers between devices, on_device(): weight_hi = lax.all_gather(head_weight[:, half:], 'dp', axis=0, tiled=True)  74.8 us
    all_gather x1, waiting for transfers between devices, on_device(): all_hi = lax.all_gather(grad_hi, 'dp', axis=0, tiled=True)  70.6 us
    all_gather x1, waiting for transfers between devices, on_device(): weight_lo = lax.all_gather(head_weight[:, :half], 'dp', axis=0, tiled=True)  52.3 us
    all_gather x1, blocking collectives, on_device(): rows_full = lax.all_gather(hidden, 'vocab', axis=1, tiled=True)  29.9 us
    all_to_all x1, waiting for transfers between devices, on_device(): lax.all_to_all(rows_full, 'dp', split_axis=1, concat_axis=0, tiled=True)  29.5 us
    all_gather x1, waiting for transfers between devices, on_device(): all_lo = lax.all_gather(grad_lo, 'dp', axis=0, tiled=True)  15.8 us
    all_to_all x2, waiting for transfers between devices, to_all(): return lax.all_to_all(copies, axis, 0, 0, tiled=True)  15.2 us
    all_to_all x2, starting transfers between devices, to_all(): return lax.all_to_all(copies, axis, 0, 0, tiled=True)  13.8 us
  transfers between devices with their start and end apart: 8, of which 8 were waited for; matrix products, arithmetic and copies ran while one was open for 5% of the time, Pallas kernels for 0%

commit v1 on v0

--- a/solution.py
+++ b/solution.py
@@ -107,7 +107,10 @@
     hidden_grad = jnp.sum(terms.astype(f32), axis=0).astype(bf16)
     objectives = to_all(jnp.full((8, 128), group_objective, f32), "dp").reshape(n_dp, 8, 128)
     loss_value = jnp.sum(objectives[:, 0, 0]) / (rows * n_dp)
-    grad_cols = lax.all_to_all(rows_full, "dp", split_axis=1, concat_axis=0, tiled=True)
+    grad_cols = jnp.concatenate(
+        lax.all_to_all(jnp.stack(jnp.split(rows_full, lax.axis_size("dp"), axis=1)), "dp", 0, 0),
+        axis=0,
+    )
     tn = (((0,), (0,)), ((), ()))
     head_grad = jnp.concatenate(
         [

time: 375 us -> 379 us (1.011)
  the two profiles are of different devices: /device:TPU:2 before, /device:TPU:4 now
where the time goes in v1:
time: 379 us; the launch traced here: 378 us
  waiting for transfers between devices  268 us (71%)
  blocking collectives  26.3 us (7%)
  starting transfers between devices  25.9 us (7%)
  matrix products  17.2 us (5%)
  between operations  17.1 us (5%)
  local copies, waits for them, and re-layouts  17 us (4%)
  other arithmetic  6.86 us (2%)
    all_gather x1, waiting for transfers between devices, on_device(): weight_hi = lax.all_gather(head_weight[:, half:], 'dp', axis=0, tiled=True)  74.9 us
    all_gather x1, waiting for transfers between devices, on_device(): all_hi = lax.all_gather(grad_hi, 'dp', axis=0, tiled=True)  74.4 us
    all_gather x1, waiting for transfers between devices, on_device(): weight_lo = lax.all_gather(head_weight[:, :half], 'dp', axis=0, tiled=True)  56 us
    all_to_all x1, waiting for transfers between devices, on_device(): lax.all_to_all(jnp.stack(jnp.split(rows_full, lax.axis_size('dp'), axis=1...  32.5 us
    all_gather x1, blocking collectives, on_device(): rows_full = lax.all_gather(hidden, 'vocab', axis=1, tiled=True)  26.3 us
    all_to_all x2, starting transfers between devices, to_all(): return lax.all_to_all(copies, axis, 0, 0, tiled=True)  14.8 us
    all_to_all x2, waiting for transfers between devices, to_all(): return lax.all_to_all(copies, axis, 0, 0, tiled=True)  12.6 us
    unnamed x41, local copies, waits for them, and re-layouts  11 us
  transfers between devices with their start and end apart: 8, of which 8 were waited for; matrix products, arithmetic and copies ran while one was open for 7% of the time, Pallas kernels for 0%

profile of v1, /device:TPU:4, one launch (start us, length us, event | category | flops | bytes accessed | tf_op | source)
XLA Modules:
  0.0 378.1 jit_solution(13991686635389292842)
XLA Ops:
  7.2 1.8 fusion.20
  9.1 0.7 all-gather.7.cloned.1.call-update
  9.8 1.2 reduce_max.71
  11.0 26.3 %all_gather.15 = bf16[128,2048]{0,1:T(8,128)(2,1)S(1)} all-gather(bf16[128,64]{0,1:T(8,128)(2,1)} %param.6), channel_id=1, replica_groups=mesh['vocab'=32,'dp'=16] {'vocab'}, dimensions={1}, use_global_device_ids=true | all-gather | bytes 540672 | tf_op jit(solution)/shard_map/all_gather | solution.py:37
  37.3 56.0 %all-gather.5.cloned.1.call-done = bf16[2048,1024]{1,0:T(8,128)(2,1)} async-done(((bf16[128,1024]{1,0:T(8,128)(2,1)}), bf16[2048,1024]{1,0:T(8,128)(2,1)}) %all-gather.5.cloned.1.call-update) | async-done | bytes 4194320 | tf_op jit(solution)/shard_map/all_gather | solution.py:40
  93.3 3.0 fusion.23
  96.4 74.9 %all-gather.7.cloned.1.call-done = bf16[2048,1024]{1,0:T(8,128)(2,1)} async-done(((bf16[128,1024]{1,0:T(8,128)(2,1)}), bf16[2048,1024]{1,0:T(8,128)(2,1)}) %all-gather.7.cloned.1.call-update) | async-done | bytes 4194320 | tf_op jit(solution)/shard_map/all_gather | solution.py:41
  171.3 3.0 fusion.24
  174.3 0.8 fusion.1
  175.2 0.7 broadcast_in_dim.8
  175.9 7.4 %all-to-all-start = ((f32[32,8,128]{2,1,0:T(8,128)}), f32[32,8,128]{2,1,0:T(8,128)S(1)}, u32[]{:S(2)}, u32[]{:S(2)}) async-start(f32[32,8,128]{2,1,0:T(8,128)} %broadcast_in_dim.8), calls=%async_computation | async-start | bytes 262144 | tf_op jit(solution)/shard_map/all_to_all | solution.py:32
  183.5 5.6 %all-to-all-done = f32[32,8,128]{2,1,0:T(8,128)S(1)} async-done(((f32[32,8,128]{2,1,0:T(8,128)}), f32[32,8,128]{2,1,0:T(8,128)S(1)}, u32[]{:S(2)}, u32[]{:S(2)}) %all-to-all-start) | async-done | bytes 131104 | tf_op jit(solution)/shard_map/all_to_all | solution.py:32
  189.3 0.6 add_reduce_fusion
  190.0 0.2 select_reduce_fusion.2
  190.2 0.6 fusion.14
  191.1 0.6 fusion.5
  191.7 0.9 fusion.18
  192.6 0.5 all-gather.11.cloned.1.call-update
  193.3 0.1 copy.93
  193.4 0.1 copy.92
  193.6 0.1 copy.91
  193.7 0.1 copy.90
  193.8 0.1 copy.89
  193.9 0.1 copy.88
  194.1 0.1 copy.87
  194.2 0.1 copy.86
  194.3 0.1 copy.85
  194.4 0.1 copy.84
  194.6 0.1 copy.83
  194.7 0.1 copy.82
  194.8 0.1 copy.81
  194.9 0.6 constant_dynamic-update-slice_fusion.15
  195.6 0.6 constant_dynamic-update-slice_fusion.14
  196.2 0.6 constant_dynamic-update-slice_fusion.13
  196.8 0.6 constant_dynamic-update-slice_fusion.12
  197.4 0.6 constant_dynamic-update-slice_fusion.11
  198.0 0.6 constant_dynamic-update-slice_fusion.10
  198.6 0.6 constant_dynamic-update-slice_fusion.9
  199.2 0.6 constant_dynamic-update-slice_fusion.8
  199.8 0.6 constant_dynamic-update-slice_fusion.7
  200.4 0.6 constant_dynamic-update-slice_fusion.6
  201.0 0.6 constant_dynamic-update-slice_fusion.5
  201.6 0.6 constant_dynamic-update-slice_fusion.4
  202.2 0.6 constant_dynamic-update-slice_fusion.3
  204.1 0.6 broadcast_in_dim_broadcast_in_dim_broadcast_in_dim.3
  204.8 7.4 %all-to-all-start.3 = ((f32[16,8,128]{2,1,0:T(8,128)}), f32[16,8,128]{2,1,0:T(8,128)S(1)}, u32[]{:S(2)}, u32[]{:S(2)}) async-start(f32[16,8,128]{2,1,0:T(8,128)} %broadcast_in_dim_broadcast_in_dim_broadcast_in_dim.3), calls=%async_computation.3 | async-start | bytes 131072 | tf_op jit(solution)/shard_map/all_to_all | solution.py:32
  212.2 3.9 %fusion.16 = f32[128,2048]{1,0:T(8,128)S(1)} fusion(bf16[2048,1024]{1,0:T(8,128)(2,1)} %all-gather.5.cloned.1.call-done, bf16[128,2048]{1,0:T(8,128)(2,1)S(1)} %fusion.5), kind=kOutput, calls=%fused_computation.64 | convolution fusion | flops 536870912 | bytes 5505024 | tf_op jit(solution)/shard_map/dot_general | solution.py:101
  216.1 1.5 fusion
  217.6 1.0 copy.59
  218.6 7.0 %all-to-all-done.3 = f32[16,8,128]{2,1,0:T(8,128)S(1)} async-done(((f32[16,8,128]{2,1,0:T(8,128)}), f32[16,8,128]{2,1,0:T(8,128)S(1)}, u32[]{:S(2)}, u32[]{:S(2)}) %all-to-all-start.3) | async-done | bytes 65568 | tf_op jit(solution)/shard_map/all_to_all | solution.py:32
  225.6 6.0 %all-to-all-start.1 = ((bf16[32,128,64]{1,2,0:T(8,128)(2,1)}), bf16[32,128,64]{1,2,0:T(8,128)(2,1)S(1)}, u32[]{:S(2)}, u32[]{:S(2)}) async-start(bf16[32,128,64]{1,2,0:T(8,128)(2,1)} %bitcast.16), calls=%async_computation.1 | async-start | bytes 1048576 | tf_op jit(solution)/shard_map/all_to_all | solution.py:106
  231.6 0.6 constant_dynamic-update-slice_fusion.2
  232.5 0.6 constant_dynamic-update-slice_fusion.1
  233.1 0.6 constant_dynamic-update-slice_fusion
  233.7 7.4 %all-to-all-done.1 = bf16[32,128,64]{1,2,0:T(8,128)(2,1)S(1)} async-done(((bf16[32,128,64]{1,2,0:T(8,128)(2,1)}), bf16[32,128,64]{1,2,0:T(8,128)(2,1)S(1)}, u32[]{:S(2)}, u32[]{:S(2)}) %all-to-all-start.1) | async-done | bytes 524320 | tf_op jit(solution)/shard_map/all_to_all | solution.py:106
  241.1 4.9 %all-to-all-start.2 = ((bf16[16,128,128]{2,1,0:T(8,128)(2,1)}), bf16[16,128,128]{2,1,0:T(8,128)(2,1)S(1)}, u32[]{:S(2)}, u32[]{:S(2)}) async-start(bf16[16,128,128]{2,1,0:T(8,128)(2,1)} %constant_dynamic-update-slice_fusion), calls=%async_computation.2 | async-start | bytes 1048576 | tf_op jit(solution)/shard_map/all_to_all | solution.py:111
  246.1 0.6 slice_reduce_fusion
  247.3 0.7 reduce_sum.188
  248.0 32.5 %all-to-all-done.2 = bf16[16,128,128]{2,1,0:T(8,128)(2,1)S(1)} async-done(((bf16[16,128,128]{2,1,0:T(8,128)(2,1)}), bf16[16,128,128]{2,1,0:T(8,128)(2,1)S(1)}, u32[]{:S(2)}, u32[]{:S(2)}) %all-to-all-start.2) | async-done | bytes 524320 | tf_op jit(solution)/shard_map/all_to_all | solution.py:111
  280.5 8.6 %all-gather.9.cloned.1.call-done = bf16[2048,1024]{1,0:T(8,128)(2,1)} async-done(((bf16[128,1024]{1,0:T(8,128)(2,1)}), bf16[2048,1024]{1,0:T(8,128)(2,1)}) %all-gather.9.cloned.1.call-update) | async-done | bytes 4194320 | tf_op jit(solution)/shard_map/all_gather | solution.py:97
  289.1 2.9 fusion.25
  292.0 74.4 %all-gather.11.cloned.1.call-done = bf16[2048,1024]{1,0:T(8,128)(2,1)} async-done(((bf16[128,1024]{1,0:T(8,128)(2,1)}), bf16[2048,1024]{1,0:T(8,128)(2,1)}) %all-gather.11.cloned.1.call-update) | async-done | bytes 4194320 | tf_op jit(solution)/shard_map/all_gather | solution.py:98
  366.4 2.9 fusion.26
  369.3 1.1 pad_maximum_fusion.1
  (36 shorter events, 1.3 us)
Async XLA Ops:
  7.2 86.2 %all-gather.5.cloned.1.call-start = ((), (), s32[]{:S(2)}) async-start(), calls=%async_computation.4 | async-start | bytes 4456448 | tf_op jit(solution)/shard_map/all_gather | solution.py:40
  9.1 162.2 %all-gather.7.cloned.1.call-start = ((), (), s32[]{:S(2)}) async-start(), calls=%async_computation.5 | async-start | bytes 4456448 | tf_op jit(solution)/shard_map/all_gather | solution.py:41
  37.3 137.0 %copy-start.1 = (bf16[128,2048]{1,0:T(8,128)(2,1)S(1)}, bf16[128,2048]{1,0:T(8,128)(2,1)}, u32[]{:S(2)}) copy-start(bf16[128,2048]{1,0:T(8,128)(2,1)} %param.8) | copy-start | bytes 1572868
  37.3 137.0 %copy-start.2 = (s32[128]{0:T(128)S(1)}, s32[128]{0:T(128)}, u32[]{:S(2)}) copy-start(s32[128]{0:T(128)} %param.9) | copy-start | bytes 1540
  96.3 87.0 %copy-start.3 = (s32[1,16]{1,0:T(1,128)S(1)}, s32[1,16]{1,0:T(1,128)}, u32[]{:S(2)}) copy-start(s32[1,16]{1,0:T(1,128)} %param.11) | copy-start | bytes 196
  96.4 93.6 %copy-start.4 = (s32[1,128]{1,0:T(1,128)S(1)}, s32[1,128]{1,0:T(1,128)}, u32[]{:S(2)}) copy-start(s32[1,128]{1,0:T(1,128)} %param.10) | copy-start | bytes 1540
  175.9 13.2 %all-to-all-start = ((f32[32,8,128]{2,1,0:T(8,128)}), f32[32,8,128]{2,1,0:T(8,128)S(1)}, u32[]{:S(2)}, u32[]{:S(2)}) async-start(f32[32,8,128]{2,1,0:T(8,128)} %broadcast_in_dim.8), calls=%async_computation | async-start | bytes 262144 | tf_op jit(solution)/shard_map/all_to_all | solution.py:32
  183.3 105.8 %all-gather.9.cloned.1.call-start = ((), (), s32[]{:S(2)}) async-start(), calls=%async_computation.6 | async-start | bytes 4456448 | tf_op jit(solution)/shard_map/all_gather | solution.py:97
  192.6 173.9 %all-gather.11.cloned.1.call-start = ((), (), s32[]{:S(2)}) async-start(), calls=%async_computation.7 | async-start | bytes 4456448 | tf_op jit(solution)/shard_map/all_gather | solution.py:98
  204.8 20.8 %all-to-all-start.3 = ((f32[16,8,128]{2,1,0:T(8,128)}), f32[16,8,128]{2,1,0:T(8,128)S(1)}, u32[]{:S(2)}, u32[]{:S(2)}) async-start(f32[16,8,128]{2,1,0:T(8,128)} %broadcast_in_dim_broadcast_in_dim_broadcast_in_dim.3), calls=%async_computation.3 | async-start | bytes 131072 | tf_op jit(solution)/shard_map/all_to_all | solution.py:32
  212.2 3.9 %copy-start = (bf16[2048,1024]{1,0:T(8,128)(2,1)S(1)}, bf16[2048,1024]{1,0:T(8,128)(2,1)}, u32[]{:S(2)}) copy-start(bf16[2048,1024]{1,0:T(8,128)(2,1)} %all-gather.7.cloned.1.call-done) | copy-start | bytes 12582916
  225.6 15.5 %all-to-all-start.1 = ((bf16[32,128,64]{1,2,0:T(8,128)(2,1)}), bf16[32,128,64]{1,2,0:T(8,128)(2,1)S(1)}, u32[]{:S(2)}, u32[]{:S(2)}) async-start(bf16[32,128,64]{1,2,0:T(8,128)(2,1)} %bitcast.16), calls=%async_computation.1 | async-start | bytes 1048576 | tf_op jit(solution)/shard_map/all_to_all | solution.py:106
  241.1 39.4 %all-to-all-start.2 = ((bf16[16,128,128]{2,1,0:T(8,128)(2,1)}), bf16[16,128,128]{2,1,0:T(8,128)(2,1)S(1)}, u32[]{:S(2)}, u32[]{:S(2)}) async-start(bf16[16,128,128]{2,1,0:T(8,128)(2,1)} %constant_dynamic-update-slice_fusion), calls=%async_computation.2 | async-start | bytes 1048576 | tf_op jit(solution)/shard_map/all_to_all | solution.py:111
Sparse Core Ops, SparseCore 0:
  10.1 83.2 all-gather.4
  96.0 75.2 all-gather.6
  192.7 96.3 all-gather.8
  291.0 75.3 all-gather.10
